TPU v7x, 32 devices: a whole 2x2x4 slice. The times are simulated.
32 devices in a mesh: ctx: 16 (over z, y, core), head: 2 (over x).
Axes of the slice: x: 2, y: 2, z: 4, core: 2. Of those that a mesh axis runs over, the one named last changes fastest.
Arguments:
- queries: bfloat16 [768, 8192], P('ctx', 'head'), may hold values from -120 to 120
- cached_keys: bfloat16 [5120, 1024], P('ctx', 'head'), may hold values from -5 to 15
- cached_values: bfloat16 [5120, 1024], P('ctx', 'head'), may hold values from -6 to 6
- fresh_keys: bfloat16 [768, 1024], P('ctx', 'head'), may hold values from -5 to 15
- fresh_values: bfloat16 [768, 1024], P('ctx', 'head'), may hold values from -6 to 6
- recompute_index: int32 [16, 48], P('ctx'), may hold values from 0 to 319, as said below
- recompute_count: int32 [16], P('ctx'), may hold values from 1 to 48, 672 in all
- group_offsets: int32 [16], replicated, may hold values from 0 to 9585, as said below
Outputs:
- attention: bfloat16 [768, 8192], P('ctx', 'head')
- joined_keys: bfloat16 [5120, 1024], P('ctx', 'head')
- joined_values: bfloat16 [5120, 1024], P('ctx', 'head')
- drift: float32 [16, 48], P('ctx')
Inputs may be any that keep to these rules, and one draw needn't show every extreme that they name: `recompute_index`: the entries of one group's row are different token numbers of that group. group_offsets[c + 1] - group_offsets[c] lies between 320 and 639.
All inputs are finite; a program needn't handle non-finite values. No bound on the sum of `recompute_count` on one device may be relied on, other than what follows from the above.
Results may differ from a plain program's by a relative error of at most 0.008.
Values may be sent and summed in bfloat16 or wider, within the bound.
A program may use at most 64 MiB of HBM per device.

v0:
```python
import math

import jax
import jax.numpy as jnp
from jax import lax
from jax.sharding import PartitionSpec as P

HEADS = 64
KV_HEADS = 8
HEAD_DIM = 128


NEG_FILL = -1e30
BLOCK_TOKENS = 2560


def inverse_freq():
    half_dim = HEAD_DIM // 2
    exponent = jnp.arange(half_dim, dtype=jnp.float32) * 2.0 / HEAD_DIM
    base_freq = 1.0 / 500000.0**exponent
    wavelength = 2.0 * jnp.pi / base_freq
    smooth = (8192.0 / wavelength - 1.0) / 3.0
    blended_freq = (1.0 - smooth) * base_freq / 8.0 + smooth * base_freq
    return jnp.where(
        wavelength < 2048.0,
        base_freq,
        jnp.where(wavelength > 8192.0, base_freq / 8.0, blended_freq),
    )


def rotate(values, positions):
    row_count = values.shape[0]
    head_count = values.shape[1] // HEAD_DIM
    half_dim = HEAD_DIM // 2
    angles = positions.astype(jnp.float32)[:, None] * inverse_freq()[None, :]
    cosine = jnp.cos(angles)[:, None, :]
    sine_part = jnp.sin(angles)[:, None, :]
    pieces_f = values.astype(jnp.float32).reshape(row_count, head_count, HEAD_DIM)
    first_half = pieces_f[:, :, :half_dim]
    second_half = pieces_f[:, :, half_dim:]
    turned = jnp.concatenate(
        [
            first_half * cosine - second_half * sine_part,
            second_half * cosine + first_half * sine_part,
        ],
        axis=2,
    )
    return turned.reshape(row_count, head_count * HEAD_DIM)


def empty_state(kv_local, row_count):
    return (
        jnp.full((kv_local, row_count), NEG_FILL, jnp.float32),
        jnp.zeros((kv_local, row_count), jnp.float32),
        jnp.zeros((kv_local, row_count, HEAD_DIM), jnp.float32),
    )


def attend(status, queries, query_pos, key_rows, value_rows, key_pos):
    maxima, totals, weighted = status
    scores = jnp.einsum("hqd,khd->hqk", queries, key_rows, preferred_element_type=jnp.float32) * (
        1.0 / math.sqrt(HEAD_DIM)
    )
    visible = key_pos[None, None, :] <= query_pos[None, :, None]
    block_peak = jnp.max(jnp.where(visible, scores, NEG_FILL), axis=2)
    raised = jnp.maximum(maxima, block_peak)
    weights = jnp.where(visible, jnp.exp(scores - raised[:, :, None]), 0.0)
    shrink = jnp.exp(maxima - raised)
    totals = totals * shrink + jnp.sum(weights, axis=2)
    weighted = weighted * shrink[:, :, None] + jnp.einsum(
        "hqk,khd->hqd", weights.astype(jnp.bfloat16), value_rows, preferred_element_type=jnp.float32
    )
    return (raised, totals, weighted)


def finish(status, tokens, heads_per):
    weighted = status[2]
    kv_local = weighted.shape[0]
    normalized = weighted / status[1][:, :, None]
    return (
        normalized.reshape(kv_local, tokens, heads_per, HEAD_DIM)
        .transpose(1, 0, 2, 3)
        .reshape(tokens, kv_local * heads_per * HEAD_DIM)
    )


def block_groups(groups_in, group_len):
    best = 1
    for count in range(1, groups_in + 1):
        if groups_in % count == 0 and count * group_len <= max(BLOCK_TOKENS, group_len):
            best = count
    return best


def fold_keys(group_offsets, group_len, query_sets):

    def absorb(running, piece, start):
        key_rows, value_rows = piece
        row_count = key_rows.shape[0]
        kv_local = key_rows.shape[1] // HEAD_DIM
        groups_in = row_count // group_len
        groups_each = block_groups(groups_in, group_len)
        block_count = groups_in // groups_each
        key_blocks = key_rows.reshape(block_count, groups_each * group_len, kv_local, HEAD_DIM)
        value_blocks = value_rows.reshape(block_count, groups_each * group_len, kv_local, HEAD_DIM)
        first_group = start // group_len

        def advance(current_states, block_item):
            key_block, value_block, number = block_item
            lead_group = number * groups_each
            group_starts = lax.dynamic_slice_in_dim(group_offsets, lead_group, groups_each)
            key_pos = (
                group_starts[:, None] + jnp.arange(group_len, dtype=jnp.int32)[None, :]
            ).reshape(-1)
            updated = []
            for status, query_set in zip(current_states, query_sets):
                updated.append(
                    lax.cond(
                        lead_group <= query_set[2],
                        lambda current: attend(
                            current, query_set[0], query_set[1], key_block, value_block, key_pos
                        ),
                        lambda current: current,
                        status,
                    )
                )
            return (tuple(updated), None)

        result_states, _ = lax.scan(
            advance, running, (key_blocks, value_blocks, jnp.arange(block_count, dtype=jnp.int32))
        )
        return result_states

    return absorb


def shards(
    queries,
    cached_keys,
    cached_values,
    fresh_keys,
    fresh_values,
    recompute_index,
    recompute_count,
    group_offsets,
):
    group_len = cached_keys.shape[0]
    rows_dev = queries.shape[0]
    kv_local = cached_keys.shape[1] // HEAD_DIM
    heads_per = HEADS // KV_HEADS
    own_group = lax.axis_index("ctx")
    own_start = lax.dynamic_index_in_dim(group_offsets, own_group, keepdims=False)
    indices = recompute_index[0]
    live_rows = jnp.arange(rows_dev, dtype=jnp.int32) < recompute_count[0]
    turned = rotate(cached_keys, own_start + jnp.zeros((group_len,), jnp.int32)).astype(
        jnp.bfloat16
    )
    fresh_turned = rotate(fresh_keys, own_start + indices).astype(jnp.bfloat16)
    picker = (jnp.arange(group_len, dtype=jnp.int32)[:, None] == indices[None, :]) & live_rows[
        None, :
    ]
    covered = jnp.any(picker, axis=1)[:, None]
    picker = picker.astype(jnp.bfloat16)
    joined_keys = jnp.where(
        covered,
        jnp.dot(picker, fresh_turned, preferred_element_type=jnp.float32),
        turned.astype(jnp.float32),
    ).astype(jnp.bfloat16)
    joined_values = jnp.where(
        covered,
        jnp.dot(picker, fresh_values, preferred_element_type=jnp.float32),
        cached_values.astype(jnp.float32),
    ).astype(jnp.bfloat16)
    key_gap = fresh_turned.astype(jnp.float32) - jnp.take(turned, indices, axis=0).astype(
        jnp.float32
    )
    value_gap = fresh_values.astype(jnp.float32) - jnp.take(cached_values, indices, axis=0).astype(
        jnp.float32
    )
    local_drift = jnp.sum(key_gap * key_gap + value_gap * value_gap, axis=1)
    kv_drift = lax.psum(local_drift, "head") / (2.0 * KV_HEADS * HEAD_DIM)
    kv_drift = jnp.where(live_rows, kv_drift, 0.0)[None, :]
    query_pos = own_start + indices
    turned_queries = rotate(queries, query_pos).astype(jnp.bfloat16)
    query_grid = (
        turned_queries.reshape(rows_dev, kv_local, heads_per, HEAD_DIM)
        .transpose(1, 0, 2, 3)
        .reshape(kv_local, rows_dev * heads_per, HEAD_DIM)
    )
    grid_pos = jnp.repeat(query_pos, heads_per)
    absorb = fold_keys(group_offsets, group_len, ((query_grid, grid_pos, own_group),))
    (own_state,) = absorb(
        (empty_state(kv_local, rows_dev * heads_per),),
        (
            lax.all_gather(joined_keys, "ctx", axis=0, tiled=True),
            lax.all_gather(joined_values, "ctx", axis=0, tiled=True),
        ),
        jnp.int32(0),
    )
    attended = finish(own_state, rows_dev, heads_per).astype(jnp.bfloat16)
    attention = jnp.where(live_rows[:, None], attended, jnp.zeros((), jnp.bfloat16))
    return (attention, joined_keys, joined_values, kv_drift)


def solution(mesh):
    return jax.shard_map(
        shards,
        mesh=mesh,
        in_specs=(
            P("ctx", "head"),
            P("ctx", "head"),
            P("ctx", "head"),
            P("ctx", "head"),
            P("ctx", "head"),
            P("ctx", None),
            P("ctx"),
            P(),
        ),
        out_specs=(P("ctx", "head"), P("ctx", "head"), P("ctx", "head"), P("ctx", None)),
        check_vma=False,
    )
```

profile of v0, /device:TPU:24, one launch (start us, length us, event | category | flops | bytes accessed | tf_op | source)
XLA Modules:
  0.0 208.2 jit_solution(6499532751974038271)
XLA Ops:
  7.9 0.8 fusion.30
  8.6 2.1 %fusion.25 = bf16[320,512]{1,0:T(8,128)(2,1)} fusion(bf16[48,512]{1,0:T(8,128)(2,1)} %param.18, bf16[320,512]{1,0:T(8,128)(2,1)} %param.16, pred[320]{0:T(512)(128)(4,1)S(1)} %fusion.30, s32[48]{0:T(128)} %bitcast.74, pred[48]{0:T(512)(128)(4,1)S(1)} %iota_compare_fusion.1), kind=kOutput, calls=%fused_computation.29 | convolution fusion | flops 16250880 | bytes 705072 | tf_op jit(solution)/shard_map/dot_general | solution.py:171
  10.8 1.2 dynamic_slice.31
  12.7 0.8 reshape.222
  13.5 1.1 copy.31
  14.8 0.2 subtract_convert_fusion.1
  15.0 0.2 copy.32
  15.2 1.3 fusion.37
  16.5 0.2 multiply_cosine_fusion
  16.7 0.1 subtract_convert_fusion.2
  16.8 0.1 pad_maximum_fusion.1
  16.9 1.8 fusion.24
  18.7 1.7 gather_fusion.1
  20.4 0.7 gather_fusion
  21.1 1.1 convert_bitcast_fusion
  22.1 0.1 copy.40
  22.3 0.7 compare_and_fusion
  23.0 1.0 add_reduce_fusion
  24.0 5.1 %psum.7 = f32[48]{0:T(128)S(1)} all-reduce(f32[48]{0:T(128)S(1)} %add_reduce_fusion), channel_id=1, replica_groups=mesh['ctx'=16,'head'=2] {'head'}, use_global_device_ids=true, to_apply=%region_8.10 | all-reduce | flops 48 | bytes 384 | tf_op jit(solution)/shard_map/psum | solution.py:181
  29.1 0.4 subtract_convert_fusion
  29.5 0.2 copy_bitcast_fusion
  29.7 0.5 select_bitcast_fusion
  30.2 36.2 %all-gather.5.cloned.1.call-done = bf16[5120,512]{1,0:T(8,128)(2,1)} async-done(((bf16[320,512]{1,0:T(8,128)(2,1)}), bf16[5120,512]{1,0:T(8,128)(2,1)}) %all-gather.5.cloned.1.call-update) | async-done | bytes 5242896 | tf_op jit(solution)/shard_map/all_gather | solution.py:196
  66.4 8.3 %reshape.220 = bf16[2,2560,4,128]{3,2,1,0:T(4,128)(2,1)} reshape(bf16[5120,512]{1,0:T(8,128)(2,1)} %all-gather.5.cloned.1.call-done) | data formatting | bytes 10485760 | tf_op jit(solution)/shard_map/reshape | solution.py:105
  74.8 5.5 %copy.35 = bf16[2,2560,4,128]{3,1,2,0:T(8,128)(2,1)} copy(bf16[2,2560,4,128]{3,2,1,0:T(4,128)(2,1)} %reshape.220) | data formatting | bytes 10485760
  80.3 43.6 %all-gather.3.cloned.1.call-done = bf16[5120,512]{1,0:T(8,128)(2,1)} async-done(((bf16[320,512]{1,0:T(8,128)(2,1)}), bf16[5120,512]{1,0:T(8,128)(2,1)}) %all-gather.3.cloned.1.call-update) | async-done | bytes 5242896 | tf_op jit(solution)/shard_map/all_gather | solution.py:195
  123.9 8.3 %reshape.216 = bf16[2,2560,4,128]{3,2,1,0:T(4,128)(2,1)} reshape(bf16[5120,512]{1,0:T(8,128)(2,1)} %all-gather.3.cloned.1.call-done) | data formatting | bytes 10485760 | tf_op jit(solution)/shard_map/reshape | solution.py:104
  132.2 5.5 %copy.34 = bf16[2,2560,4,128]{3,1,2,0:T(8,128)(2,1)} copy(bf16[2,2560,4,128]{3,2,1,0:T(4,128)(2,1)} %reshape.216) | data formatting | bytes 10485760
  137.8 62.3 %while.15 = (s32[]{:T(128)}, f32[4,384]{1,0:T(4,128)S(1)}, f32[4,384]{1,0:T(4,128)S(1)}, f32[4,384,128]{2,1,0:T(8,128)S(1)}, s32[2]{0:T(128)S(1)}, /*index=5*/s3...) while((s32[]{:T(128)}, f32[4,384]{1,0:T(4,128)S(1)}, ...), condition=%wide.region_6.7_spmd.clone, body=%wide.region_1.0_spmd.clone.sunk | while | flops 2057901568 | bytes 58494592 | solution.py:129
  137.8 0.7 dynamic_slice.46
  139.1 29.8 %conditional.3 = ((f32[4,384]{1,0:T(4,128)S(1)}, f32[4,384]{1,0:T(4,128)S(1)}, f32[4,384,128]{2,1,0:T(8,128)S(1)})) conditional(s32[]{:T(128)} %convert_element_type.108, (f32[4,384]{1,0:T(4,128)S(1)}, f32[4,384]{1,0:T(4,128)S(1)}, f32[4,384,128]{2,1,0:T(8,128)S(1)}) %tuple.57, (s32[]{:T(128)}, s32[16]{0:T(128)S(1)}, s32[8,320]{1,0:T(8,128)S(1)}, ...), branch_computations={%region_2.2_spmd, %region_3.5_spmd} | conditional | flops 2057901568 | bytes 58484072 | solution.py:118
  139.1 0.1 dynamic_slice.26
  139.2 0.1 broadcast_add_fusion
  139.4 0.1 le.28
  139.5 1.2 broadcast_compare_fusion
  140.7 10.1 %fusion.2 = (f32[4,384]{1,0:T(4,128)S(1)}, f32[4,2560,384]{2,1,0:T(8,128)}) fusion(pred[384,2560]{0,1:T(8,128)(4,1)S(1)} %broadcast_compare_fusion, bf16[4,384,128]{2,1,0:T(8,128)(2,1)S(1)} %get-tuple-element.154, bf16[2,2560,4,128]{3,1,2,0:T(8,128)(2,1)} %get-tuple-element.152, s32[]{:T(128)} %get-tuple-element.153), kind=kOutput, calls=%fused_computation.5 | convolution fusion | flops 1018427904 | bytes 19732992 | tf_op jit(solution)/shard_map/while/body/eval_jaxpr/cond/branch_1_fun/hqd,khd->hqk/dot_general | solution.py:61
  150.8 8.8 %fusion.6 = f32[4,384]{1,0:T(4,128)S(1)} fusion(f32[4,2560,384]{2,1,0:T(8,128)} %get-tuple-element.292, f32[4,384]{1,0:T(4,128)S(1)} %max.4, pred[384,2560]{0,1:T(8,128)(4,1)S(1)} %broadcast_compare_fusion), kind=kLoop, calls=%fused_computation.9 | loop fusion | flops 15727104 | bytes 16723968 | tf_op jit(solution)/shard_map/while/body/eval_jaxpr/cond/branch_1_fun/reduce_sum | solution.py:69
  159.6 9.3 %fusion.15 = f32[4,384,128]{2,1,0:T(8,128)S(1)} fusion(bf16[2,2560,4,128]{3,1,2,0:T(8,128)(2,1)} %get-tuple-element.157, s32[]{:T(128)} %get-tuple-element.153, f32[4,2560,384]{2,1,0:T(8,128)} %get-tuple-element.292, f32[4,384]{1,0:T(4,128)S(1)} %max.4, pred[384,2560]{0,1:T(8,128)(4,1)S(1)} %broadcast_compare_fusion, ...), kind=kOutput, calls=%fused_computation.18 | convolution fusion | flops 1022754816 | bytes 20918784 | tf_op jit(solution)/shard_map/while/body/eval_jaxpr/cond/branch_1_fun/hqk,khd->hqd/dot_general | solution.py:70
  168.9 0.7 dynamic_slice.46
  170.2 29.8 %conditional.3 = ((f32[4,384]{1,0:T(4,128)S(1)}, f32[4,384]{1,0:T(4,128)S(1)}, f32[4,384,128]{2,1,0:T(8,128)S(1)})) conditional(s32[]{:T(128)} %convert_element_type.108, (f32[4,384]{1,0:T(4,128)S(1)}, f32[4,384]{1,0:T(4,128)S(1)}, f32[4,384,128]{2,1,0:T(8,128)S(1)}) %tuple.57, (s32[]{:T(128)}, s32[16]{0:T(128)S(1)}, s32[8,320]{1,0:T(8,128)S(1)}, ...), branch_computations={%region_2.2_spmd, %region_3.5_spmd} | conditional | flops 2057901568 | bytes 58484072 | solution.py:118
  170.3 0.1 dynamic_slice.26
  170.6 0.1 le.28
  170.7 1.2 broadcast_compare_fusion
  171.9 10.1 %fusion.2 = (f32[4,384]{1,0:T(4,128)S(1)}, f32[4,2560,384]{2,1,0:T(8,128)}) fusion(pred[384,2560]{0,1:T(8,128)(4,1)S(1)} %broadcast_compare_fusion, bf16[4,384,128]{2,1,0:T(8,128)(2,1)S(1)} %get-tuple-element.154, bf16[2,2560,4,128]{3,1,2,0:T(8,128)(2,1)} %get-tuple-element.152, s32[]{:T(128)} %get-tuple-element.153), kind=kOutput, calls=%fused_computation.5 | convolution fusion | flops 1018427904 | bytes 19732992 | tf_op jit(solution)/shard_map/while/body/eval_jaxpr/cond/branch_1_fun/hqd,khd->hqk/dot_general | solution.py:61
  182.0 8.8 %fusion.6 = f32[4,384]{1,0:T(4,128)S(1)} fusion(f32[4,2560,384]{2,1,0:T(8,128)} %get-tuple-element.292, f32[4,384]{1,0:T(4,128)S(1)} %max.4, pred[384,2560]{0,1:T(8,128)(4,1)S(1)} %broadcast_compare_fusion), kind=kLoop, calls=%fused_computation.9 | loop fusion | flops 15727104 | bytes 16723968 | tf_op jit(solution)/shard_map/while/body/eval_jaxpr/cond/branch_1_fun/reduce_sum | solution.py:69
  190.8 9.3 %fusion.15 = f32[4,384,128]{2,1,0:T(8,128)S(1)} fusion(bf16[2,2560,4,128]{3,1,2,0:T(8,128)(2,1)} %get-tuple-element.157, s32[]{:T(128)} %get-tuple-element.153, f32[4,2560,384]{2,1,0:T(8,128)} %get-tuple-element.292, f32[4,384]{1,0:T(4,128)S(1)} %max.4, pred[384,2560]{0,1:T(8,128)(4,1)S(1)} %broadcast_compare_fusion, ...), kind=kOutput, calls=%fused_computation.18 | convolution fusion | flops 1022754816 | bytes 20918784 | tf_op jit(solution)/shard_map/while/body/eval_jaxpr/cond/branch_1_fun/hqk,khd->hqd/dot_general | solution.py:70
  200.1 0.3 fusion.26
  200.5 0.9 bitcast_select_fusion.1
  (29 shorter events, 0.8 us)
Async XLA Ops:
  7.2 59.3 %all-gather.5.cloned.1.call-start = ((), (), s32[]{:S(2)}) async-start(), calls=%async_computation.1 | async-start | bytes 5570560 | tf_op jit(solution)/shard_map/all_gather | solution.py:196
  10.8 113.1 %all-gather.3.cloned.1.call-start = ((), (), s32[]{:S(2)}) async-start(), calls=%async_computation | async-start | bytes 5570560 | tf_op jit(solution)/shard_map/all_gather | solution.py:195
  74.8 63.0 %copy-start = (s32[16]{0:T(128)S(1)}, s32[16]{0:T(128)}, u32[]{:S(2)}) copy-start(s32[16]{0:T(128)} %param.21) | copy-start | bytes 196
Sparse Core Ops, SparseCore 0:
  10.9 55.5 all-gather.4
  69.3 54.5 all-gather.2
where the time goes:
time: 211 us; the launch traced here: 208 us
  waiting for transfers between devices  79.9 us (38%)
  matrix products  42.7 us (20%)
  local copies, waits for them, and re-layouts  35.6 us (17%)
  other arithmetic  27.9 us (13%)
  between operations  15.5 us (7%)
  blocking collectives  5.12 us (2%)
    all_gather x1, waiting for transfers between devices, shards(): lax.all_gather(joined_keys, 'ctx', axis=0, tiled=True)  43.6 us
    all_gather x1, waiting for transfers between devices, shards(): lax.all_gather(joined_values, 'ctx', axis=0, tiled=True)  36.2 us
    dot_general x2, matrix products, attend(): jnp.einsum('hqd,khd->hqk', queries, key_rows, preferred_element_type=jnp....  20.2 us
    dot_general x2, matrix products, attend(): jnp.einsum('hqk,khd->hqd', weights.astype(jnp.bfloat16), value_rows, pref...  18.5 us
    reduce_sum x2, other arithmetic, attend(): totals = totals * shrink + jnp.sum(weights, axis=2)  17.6 us
    unnamed x5, local copies, waits for them, and re-layouts  11.1 us
    reshape x1, local copies, waits for them, and re-layouts, absorb(): value_rows.reshape(block_count, groups_each * group_len, kv_local, HEAD_DIM)  8.33 us
    reshape x1, local copies, waits for them, and re-layouts, absorb(): key_rows.reshape(block_count, groups_each * group_len, kv_local, HEAD_DIM)  8.32 us
  transfers between devices with their start and end apart: 2, of which 2 were waited for; matrix products, arithmetic and copies ran while one was open for 13% of the time, Pallas kernels for 0%

commit v1 on v0

v1 whole, which is shorter than its diff:
```python
import functools
import math

import jax
import jax.numpy as jnp
from jax import lax
from jax.experimental import pallas as pl
from jax.experimental.pallas import tpu as pltpu
from jax.sharding import PartitionSpec as P

HEADS = 64
KV_HEADS = 8
HEAD_DIM = 128
HEADS_PER = HEADS // KV_HEADS
SCALE = math.log2(math.e) / math.sqrt(HEAD_DIM)
NEG_FILL = -1e30
LAYERS = 4
MESH = pl.DeviceIdType.MESH


def inverse_freq():
    half_dim = HEAD_DIM // 2
    exponent = jnp.arange(half_dim, dtype=jnp.float32) * 2.0 / HEAD_DIM
    base_freq = 1.0 / 500000.0**exponent
    wavelength = 2.0 * jnp.pi / base_freq
    smooth = (8192.0 / wavelength - 1.0) / 3.0
    blended_freq = (1.0 - smooth) * base_freq / 8.0 + smooth * base_freq
    return jnp.where(
        wavelength < 2048.0,
        base_freq,
        jnp.where(wavelength > 8192.0, base_freq / 8.0, blended_freq),
    )


def dot(a, b, a_dim, b_dim, precision=None):
    return lax.dot_general(
        a,
        b,
        (((a_dim,), (b_dim,)), ((), ())),
        preferred_element_type=jnp.float32,
        precision=precision,
    )


def turn(block, cosine, sine):
    x = block.astype(jnp.float32)
    return (x * cosine + pltpu.roll(x, HEAD_DIM // 2, 1) * sine).astype(jnp.bfloat16)


def kernel(
    n,
    n_head,
    q_ref,
    ck_ref,
    cv_ref,
    fk_ref,
    fv_ref,
    cos_ref,
    sin_ref,
    meta_ref,
    out_ref,
    jk_ref,
    jv_ref,
    drift_ref,
    kv_buf,
    q_all,
    m0,
    l0,
    acc0,
    m1,
    l1,
    acc1,
    po_src,
    ps_src,
    po_dst,
    ps_dst,
    d_buf,
    kv_recv,
    kv_send,
    fw_send,
    q_send,
    q_recv,
    po_send,
    po_recv,
    ps_send,
    ps_recv,
    d_send,
    d_recv,
):
    me = lax.axis_index("ctx")
    my_head = lax.axis_index("head")
    layer_size = n // LAYERS
    half = 2 * layer_size
    columns = layer_size // 2
    kv_local = kv_buf.shape[1]
    tokens = kv_buf.shape[3]
    slots = q_ref.shape[0]
    z = me // layer_size
    odd = z % 2
    mine = me % half
    y = (me % layer_size) // 2
    core = me % 2
    layer_start = z * layer_size
    below_start = layer_start - layer_size
    half_start = me - mine
    sibling = half_start + mine + 1 - 2 * core
    server = layer_size + me % layer_size

    barrier = pltpu.get_barrier_semaphore()

    def greet(target):
        pl.semaphore_signal(barrier, inc=1, device_id={"ctx": target}, device_id_type=MESH)

    greet(sibling)
    other_start = jnp.where(odd == 1, below_start, layer_start + layer_size)
    for k in range(columns):
        if k:
            greet(layer_start + lax.rem(y + k, columns) * 2 + core)
        greet(other_start + k * 2 + core)
    for k in range(1, n_head):
        pl.semaphore_signal(
            barrier,
            inc=1,
            device_id={"head": lax.rem(my_head + k, n_head)},
            device_id_type=MESH,
        )

    @pl.when(z == 1)
    def _():
        greet(me + layer_size)
        greet(me + 2 * layer_size)

    @pl.when(z >= 2)
    def _():
        greet(server)

    idx_row = meta_ref[0:1, :slots]
    live_row = meta_ref[1:2, :slots]
    base_cos = cos_ref[slots : slots + 1, :]
    base_sin = sin_ref[slots : slots + 1, :]
    slot_cos = cos_ref[:slots, :]
    slot_sin = sin_ref[:slots, :]
    hit = lax.broadcasted_iota(jnp.int32, (tokens, slots), 0) == idx_row
    hit_live = hit & (live_row > 0)
    covered = jnp.max(hit_live.astype(jnp.float32), axis=1, keepdims=True) > 0.0
    hit = hit.astype(jnp.bfloat16)
    hit_live = hit_live.astype(jnp.bfloat16)
    ones = jnp.ones((8, HEAD_DIM), jnp.float32)
    drift = jnp.zeros((8, slots), jnp.float32)
    for h in range(kv_local):
        cols = slice(h * HEAD_DIM, (h + 1) * HEAD_DIM)
        turned = turn(ck_ref[:, cols], base_cos, base_sin)
        fresh = turn(fk_ref[:, cols], slot_cos, slot_sin)
        cached_v = cv_ref[:, cols]
        fresh_v = fv_ref[:, cols]
        keys = jnp.where(
            covered, dot(hit_live, fresh, 1, 0), turned.astype(jnp.float32)
        ).astype(jnp.bfloat16)
        vals = jnp.where(
            covered, dot(hit_live, fresh_v, 1, 0), cached_v.astype(jnp.float32)
        ).astype(jnp.bfloat16)
        jk_ref[:, cols] = keys
        jv_ref[:, cols] = vals
        kv_buf[mine, h, 0] = keys
        kv_buf[mine, h, 1] = vals
        key_gap = fresh.astype(jnp.float32) - dot(hit, turned, 0, 0)
        val_gap = fresh_v.astype(jnp.float32) - dot(hit, cached_v, 0, 0)
        drift += dot(
            ones, key_gap * key_gap + val_gap * val_gap, 1, 1, lax.Precision.HIGHEST
        )
        for g in range(HEADS_PER):
            at = (h * HEADS_PER + g) * HEAD_DIM
            q_all[0, h, g * slots : (g + 1) * slots, :] = turn(
                q_ref[:, at : at + HEAD_DIM], slot_cos, slot_sin
            )
    d_buf[my_head] = jnp.zeros(d_buf.shape[1:], jnp.float32)
    d_buf[my_head, :, :slots] = drift

    extra = jnp.where(z == 0, 0, jnp.where(z == 1, 2, 1))
    pl.semaphore_wait(barrier, 2 * columns + n_head - 1 + extra)

    def copy(src, dst, send, recv, target):
        return pltpu.make_async_remote_copy(
            src_ref=src,
            dst_ref=dst,
            send_sem=send,
            recv_sem=recv,
            device_id={"ctx": target},
            device_id_type=MESH,
        )

    def kv_copy(block, h, send, target):
        return copy(kv_buf.at[block, h], kv_buf.at[block, h], send, kv_recv.at[block, h], target)

    def q_copy(h):
        which = jnp.where(z >= 2, z - 1, 1)
        return copy(
            q_all.at[0, h], q_all.at[which, h], q_send.at[h], q_recv.at[which - 1, h], server
        )

    def po_copy(k, h, target):
        return copy(po_src.at[k, h], po_dst.at[h], po_send.at[k, h], po_recv.at[h], target)

    def ps_copy(k, h, target):
        return copy(ps_src.at[k, h], ps_dst.at[h], ps_send.at[k, h], ps_recv.at[h], target)

    def each_send(h, act):
        for k in range(columns):
            @pl.when(odd == 0)
            def _():
                act(kv_copy(mine, h, kv_send.at[columns + k, h],
                            other_start + lax.rem(y + k, columns) * 2 + core))
        for k in range(1, columns):
            there = lax.rem(y + k, columns)

            @pl.when((odd == 1) | (there > y))
            def _():
                act(kv_copy(mine, h, kv_send.at[k, h], layer_start + there * 2 + core))

        @pl.when(z >= 2)
        def _():
            act(q_copy(h))

    def start_sends(h, carry):
        each_send(h, lambda c: c.start())
        return carry

    lax.fori_loop(0, kv_local, start_sends, 0)

    def drift_copy(k):
        target = lax.rem(my_head + k, n_head)
        return pltpu.make_async_remote_copy(
            src_ref=d_buf.at[my_head],
            dst_ref=d_buf.at[my_head],
            send_sem=d_send.at[k],
            recv_sem=d_recv.at[k],
            device_id={"head": target},
            device_id_type=MESH,
        )

    for k in range(1, n_head):
        drift_copy(k).start()

    idx_all = meta_ref[0:1, :]

    def scores(block, h, q):
        return dot(kv_buf[block, h, 0], q, 1, 1) * SCALE

    def update(block, h, s, m, l, acc):
        raised = jnp.maximum(m, jnp.max(s, axis=0, keepdims=True))
        p = jnp.exp2(s - raised)
        shrink = jnp.exp2(m - raised)
        l = l * shrink + jnp.sum(p, axis=0, keepdims=True)
        acc = acc * shrink + dot(kv_buf[block, h, 1], p.astype(jnp.bfloat16), 0, 0)
        return raised, l, acc

    def process(block, h):
        @pl.when(block == mine)
        def _():
            s = scores(block, h, q_all[0, h])
            token = lax.broadcasted_iota(jnp.int32, s.shape, 0)
            s = jnp.where(token <= idx_all, s, NEG_FILL)
            m0[h], l0[h], acc0[h] = update(block, h, s, m0[h], l0[h], acc0[h])

        @pl.when(block < mine)
        def _():
            s = scores(block, h, q_all[0, h])
            m0[h], l0[h], acc0[h] = update(block, h, s, m0[h], l0[h], acc0[h])

        @pl.when(z == 1)
        def _():
            for k in range(2):
                s = scores(block, h, q_all[1 + k, h])
                m1[k], l1[k], acc1[k] = update(block, h, s, m1[k], l1[k], acc1[k])

    def source(j):
        below = j // columns
        there = lax.rem(y + j % columns, columns)
        block = (odd - below) * layer_size + there * 2 + core
        need = ((odd == 1) | (below == 0)) & ((odd == 1) | (there <= y))
        return block, need

    def head_step(h, carry):
        m0[h] = jnp.full(m0.shape[1:], NEG_FILL, jnp.float32)
        l0[h] = jnp.zeros(l0.shape[1:], jnp.float32)
        acc0[h] = jnp.zeros(acc0.shape[1:], jnp.float32)

        @pl.when(z == 1)
        def _():
            m1[...] = jnp.full(m1.shape, NEG_FILL, jnp.float32)
            l1[...] = jnp.zeros(l1.shape, jnp.float32)
            acc1[...] = jnp.zeros(acc1.shape, jnp.float32)
            for k in range(2):
                copy(
                    q_all.at[0, h], q_all.at[1 + k, h], q_send.at[h], q_recv.at[k, h], server
                ).wait_recv()

        def block_step(j, inner):
            block, need = source(j)

            @pl.when(need)
            def _():
                @pl.when(block != mine)
                def _():
                    kv_copy(block, h, fw_send.at[j, h], sibling).wait_recv()

                kv_copy(block, h, fw_send.at[j, h], sibling).start()
                process(block, h)
                twin = block + 1 - 2 * core
                kv_copy(twin, h, fw_send.at[j, h], sibling).wait_recv()
                process(twin, h)

            return inner

        lax.fori_loop(0, 2 * columns, block_step, 0)

        @pl.when(z == 1)
        def _():
            for k in range(2):
                po_src[k, h] = (acc1[k] / l1[k]).astype(jnp.bfloat16)
                ps_src[k, h] = jnp.broadcast_to(m1[k] + jnp.log2(l1[k]), ps_src.shape[2:])
                po_copy(k, h, me + (1 + k) * layer_size).start()
                ps_copy(k, h, me + (1 + k) * layer_size).start()

        return carry

    lax.fori_loop(0, kv_local, head_step, 0)

    live_all = meta_ref[1:2, :] > 0

    def store(h, rows):
        rows = jnp.where(live_all, rows, 0.0).T.astype(jnp.bfloat16)
        for g in range(HEADS_PER):
            at = pl.multiple_of((h * HEADS_PER + g) * HEAD_DIM, HEAD_DIM)
            out_ref[:, pl.ds(at, HEAD_DIM)] = rows[g * slots : (g + 1) * slots, :]

    def finish(h, carry):
        @pl.when(z < 2)
        def _():
            store(h, acc0[h] / l0[h])

        @pl.when(z >= 2)
        def _():
            po_copy(0, h, server).wait_recv()
            ps_copy(0, h, server).wait_recv()
            stat = ps_dst[h, 0:1, :]
            top = jnp.maximum(m0[h], stat)
            own = jnp.exp2(m0[h] - top)
            far = jnp.exp2(stat - top)
            total = l0[h] * own + far
            store(h, acc0[h] * (own / total) + po_dst[h].astype(jnp.float32) * (far / total))

        return carry

    lax.fori_loop(0, kv_local, finish, 0)

    for k in range(1, n_head):
        drift_copy(k).wait_recv()
    summed = d_buf[0, 0:1, :slots]
    for k in range(1, n_head):
        summed = summed + d_buf[k, 0:1, :slots]
    drift_ref[...] = jnp.where(live_row > 0, summed / (2.0 * KV_HEADS * HEAD_DIM), 0.0)
    for k in range(1, n_head):
        drift_copy(k).wait_send()

    def drain(h, carry):
        each_send(h, lambda c: c.wait_send())

        def drain_block(j, inner):
            block, need = source(j)

            @pl.when(need)
            def _():
                kv_copy(block, h, fw_send.at[j, h], sibling).wait_send()

            return inner

        lax.fori_loop(0, 2 * columns, drain_block, 0)

        @pl.when(z == 1)
        def _():
            for k in range(2):
                po_copy(k, h, me + (1 + k) * layer_size).wait_send()
                ps_copy(k, h, me + (1 + k) * layer_size).wait_send()

        return carry

    lax.fori_loop(0, kv_local, drain, 0)


def shards(
    n,
    n_head,
    queries,
    cached_keys,
    cached_values,
    fresh_keys,
    fresh_values,
    recompute_index,
    recompute_count,
    group_offsets,
):
    tokens, width = cached_keys.shape
    slots = queries.shape[0]
    kv_local = width // HEAD_DIM
    own_start = lax.dynamic_index_in_dim(group_offsets, lax.axis_index("ctx"), keepdims=False)
    indices = recompute_index[0]
    live = (jnp.arange(slots, dtype=jnp.int32) < recompute_count[0]).astype(jnp.int32)
    positions = own_start + jnp.concatenate([indices, jnp.zeros((8,), jnp.int32)])
    angles = positions.astype(jnp.float32)[:, None] * inverse_freq()[None, :]
    cosine = jnp.cos(angles)
    sine = jnp.sin(angles)
    cosine = jnp.concatenate([cosine, cosine], axis=1)
    sine = jnp.concatenate([-sine, sine], axis=1)
    meta = jnp.stack([jnp.tile(indices, HEADS_PER), jnp.tile(live, HEADS_PER)])
    rows = slots * HEADS_PER
    half = n // 2
    columns = n // LAYERS // 2
    bf16, f32 = jnp.bfloat16, jnp.float32
    dma = pltpu.SemaphoreType.DMA
    return pl.pallas_call(
        functools.partial(kernel, n, n_head),
        out_shape=(
            jax.ShapeDtypeStruct(queries.shape, bf16),
            jax.ShapeDtypeStruct(cached_keys.shape, bf16),
            jax.ShapeDtypeStruct(cached_values.shape, bf16),
            jax.ShapeDtypeStruct((1, slots), f32),
        ),
        in_specs=[pl.BlockSpec(memory_space=pltpu.VMEM)] * 8,
        out_specs=(pl.BlockSpec(memory_space=pltpu.VMEM),) * 4,
        scratch_shapes=[
            pltpu.VMEM((half, kv_local, 2, tokens, HEAD_DIM), bf16),
            pltpu.VMEM((3, kv_local, rows, HEAD_DIM), bf16),
            pltpu.VMEM((kv_local, 1, rows), f32),
            pltpu.VMEM((kv_local, 1, rows), f32),
            pltpu.VMEM((kv_local, HEAD_DIM, rows), f32),
            pltpu.VMEM((2, 1, rows), f32),
            pltpu.VMEM((2, 1, rows), f32),
            pltpu.VMEM((2, HEAD_DIM, rows), f32),
            pltpu.VMEM((2, kv_local, HEAD_DIM, rows), bf16),
            pltpu.VMEM((2, kv_local, 8, rows), f32),
            pltpu.VMEM((kv_local, HEAD_DIM, rows), bf16),
            pltpu.VMEM((kv_local, 8, rows), f32),
            pltpu.VMEM((n_head, 8, HEAD_DIM), f32),
            dma((half, kv_local)),
            dma((2 * columns, kv_local)),
            dma((2 * columns, kv_local)),
            dma((kv_local,)),
            dma((2, kv_local)),
            dma((2, kv_local)),
            dma((kv_local,)),
            dma((2, kv_local)),
            dma((kv_local,)),
            dma((n_head,)),
            dma((n_head,)),
        ],
        compiler_params=pltpu.CompilerParams(
            collective_id=0, has_side_effects=True, vmem_limit_bytes=40 * 1024 * 1024
        ),
        cost_estimate=pl.CostEstimate(
            flops=4 * half * kv_local * tokens * rows * HEAD_DIM,
            bytes_accessed=8 * tokens * width,
            transcendentals=half * kv_local * tokens * rows,
        ),
    )(queries, cached_keys, cached_values, fresh_keys, fresh_values, cosine, sine, meta)


def solution(mesh):
    return jax.shard_map(
        functools.partial(shards, mesh.shape["ctx"], mesh.shape["head"]),
        mesh=mesh,
        in_specs=(
            P("ctx", "head"),
            P("ctx", "head"),
            P("ctx", "head"),
            P("ctx", "head"),
            P("ctx", "head"),
            P("ctx", None),
            P("ctx"),
            P(),
        ),
        out_specs=(P("ctx", "head"), P("ctx", "head"), P("ctx", "head"), P("ctx", None)),
        check_vma=False,
    )
```

time: 211 us -> 80.3 us (0.38)
  the two profiles are of different devices: /device:TPU:24 before, /device:TPU:29 now
where the time goes in v1:
time: 80.3 us; the launch traced here: 80 us
  Pallas kernels  69.3 us (86%)
  local copies, waits for them, and re-layouts  8.4 us (10%)
  between operations  1.37 us (2%)
  other arithmetic  0.95 us (1%)
    pallas_call x1, Pallas kernels, shards(): pl.pallas_call(functools.partial(kernel, n, n_head), out_shape=(jax.Shape...  69.3 us
    unnamed x18, local copies, waits for them, and re-layouts  7.66 us

profile of v1, /device:TPU:29, one launch (start us, length us, event | category | flops | bytes accessed | tf_op | source)
XLA Modules:
  0.0 80.0 jit_solution(13664908841025190818)
XLA Ops:
  1.3 0.0 copy-start.6
  1.3 0.6 copy-done.6
  1.9 0.6 dynamic_slice.4
  2.5 0.0 copy-start.5
  2.5 0.7 copy-done.5
  3.2 0.6 add_convert_fusion
  3.9 0.1 stack_tile.7
  3.9 0.1 stack_tile.6
  4.0 0.2 fusion
  4.2 0.0 copy-start.3
  4.2 0.0 copy-start.4
  4.3 0.1 pad_maximum_fusion
  4.3 0.7 copy-done.3
  5.0 0.0 copy-done.4
  5.1 0.0 copy-start
  5.1 1.0 %copy-done = bf16[48,4096]{1,0:T(8,128)(2,1)S(1)} copy-done((bf16[48,4096]{1,0:T(8,128)(2,1)S(1)}, bf16[48,4096]{1,0:T(8,128)(2,1)}, u32[]{:S(2)}) %copy-start) | copy-done | bytes 393240
  6.1 0.0 copy-start.1
  6.1 1.0 %copy-done.1 = bf16[320,512]{1,0:T(8,128)(2,1)S(1)} copy-done((bf16[320,512]{1,0:T(8,128)(2,1)S(1)}, bf16[320,512]{1,0:T(8,128)(2,1)}, u32[]{:S(2)}) %copy-start.1) | copy-done | bytes 327704
  7.0 0.0 copy-start.2
  7.0 1.0 %copy-done.2 = bf16[320,512]{1,0:T(8,128)(2,1)S(1)} copy-done((bf16[320,512]{1,0:T(8,128)(2,1)S(1)}, bf16[320,512]{1,0:T(8,128)(2,1)}, u32[]{:S(2)}) %copy-start.2) | copy-done | bytes 327704
  8.0 69.3 %shard_map.111 = (bf16[48,4096]{1,0:T(8,128)(2,1)S(1)}, bf16[320,512]{1,0:T(8,128)(2,1)S(1)}, bf16[320,512]{1,0:T(8,128)(2,1)S(1)}, f32[1,48]{1,0:T(1,128)S(1)}) custom-call(bf16[48,4096]{1,0:T(8,128)(2,1)S(1)} %copy-done, bf16[320,512]{1,0:T(8,128)(2,1)S(1)} %copy-done.1, bf16[320,512]{1,0:T(8,128)(2,1)S(1)} %copy-done.2, bf16[48,512]{1,0:T(8,128)(2,1)S(1)} %copy-done.3, ...), custom_call_target="tpu_custom_call" | custom-call | flops 2013265920 | bytes 1310720 | tf_op jit(solution)/shard_map/pallas_call | solution.py:421
  77.3 0.7 copy.17
  78.0 0.7 copy.18
  78.8 0.7 copy.19
  79.5 0.5 copy.20
  (5 shorter events, 0.0 us)
Async XLA Ops:
  1.3 0.7 copy-start.6
  2.5 0.7 copy-start.5
  4.2 0.8 %copy-start.3 = (bf16[48,512]{1,0:T(8,128)(2,1)S(1)}, bf16[48,512]{1,0:T(8,128)(2,1)}, u32[]{:S(2)}) copy-start(bf16[48,512]{1,0:T(8,128)(2,1)} %fk_ref.1) | copy-start | bytes 147460
  4.2 0.8 %copy-start.4 = (bf16[48,512]{1,0:T(8,128)(2,1)S(1)}, bf16[48,512]{1,0:T(8,128)(2,1)}, u32[]{:S(2)}) copy-start(bf16[48,512]{1,0:T(8,128)(2,1)} %fv_ref.1) | copy-start | bytes 147460
  5.1 1.0 %copy-start = (bf16[48,4096]{1,0:T(8,128)(2,1)S(1)}, bf16[48,4096]{1,0:T(8,128)(2,1)}, u32[]{:S(2)}) copy-start(bf16[48,4096]{1,0:T(8,128)(2,1)} %q_ref.1) | copy-start | bytes 1179652
  6.1 1.0 %copy-start.1 = (bf16[320,512]{1,0:T(8,128)(2,1)S(1)}, bf16[320,512]{1,0:T(8,128)(2,1)}, u32[]{:S(2)}) copy-start(bf16[320,512]{1,0:T(8,128)(2,1)} %ck_ref.1) | copy-start | bytes 983044
  7.0 1.0 %copy-start.2 = (bf16[320,512]{1,0:T(8,128)(2,1)S(1)}, bf16[320,512]{1,0:T(8,128)(2,1)}, u32[]{:S(2)}) copy-start(bf16[320,512]{1,0:T(8,128)(2,1)} %cv_ref.1) | copy-start | bytes 983044

commit v2 on v1

--- a/solution.py
+++ b/solution.py
@@ -58,6 +58,7 @@
     cos_ref,
     sin_ref,
     meta_ref,
+    wide_ref,
     out_ref,
     jk_ref,
     jv_ref,
@@ -241,37 +242,41 @@
     for k in range(1, n_head):
         drift_copy(k).start()
 
-    idx_all = meta_ref[0:1, :]
-
-    def scores(block, h, q):
-        return dot(kv_buf[block, h, 0], q, 1, 1) * SCALE
-
-    def update(block, h, s, m, l, acc):
-        raised = jnp.maximum(m, jnp.max(s, axis=0, keepdims=True))
-        p = jnp.exp2(s - raised)
+    idx_all = jnp.concatenate([wide_ref[0]] * HEADS_PER, axis=0)
+    repeats = 2 * tokens // HEAD_DIM
+
+    def update(s, v_one, m, l, acc):
+        raised = jnp.maximum(m, jnp.max(s, axis=1, keepdims=True))
+        p = jnp.exp2(s - jnp.concatenate([raised] * repeats, axis=1)).astype(jnp.bfloat16)
         shrink = jnp.exp2(m - raised)
-        l = l * shrink + jnp.sum(p, axis=0, keepdims=True)
-        acc = acc * shrink + dot(kv_buf[block, h, 1], p.astype(jnp.bfloat16), 0, 0)
+        both = dot(p, v_one, 1, 0)
+        l = l * shrink + both[:, HEAD_DIM:]
+        acc = acc * shrink + both[:, :HEAD_DIM]
         return raised, l, acc
 
-    def process(block, h):
-        @pl.when(block == mine)
-        def _():
-            s = scores(block, h, q_all[0, h])
-            token = lax.broadcasted_iota(jnp.int32, s.shape, 0)
-            s = jnp.where(token <= idx_all, s, NEG_FILL)
-            m0[h], l0[h], acc0[h] = update(block, h, s, m0[h], l0[h], acc0[h])
-
-        @pl.when(block < mine)
-        def _():
-            s = scores(block, h, q_all[0, h])
-            m0[h], l0[h], acc0[h] = update(block, h, s, m0[h], l0[h], acc0[h])
+    def process(pair, h):
+        def operands():
+            k = jnp.concatenate([kv_buf[pair, h, 0], kv_buf[pair + 1, h, 0]], axis=0)
+            v = jnp.concatenate([kv_buf[pair, h, 1], kv_buf[pair + 1, h, 1]], axis=0)
+            return k, jnp.concatenate([v, jnp.ones_like(v)], axis=1)
+
+        def own(k, v_one):
+            s = dot(q_all[0, h], k, 1, 1) * SCALE
+            token = lax.broadcasted_iota(jnp.int32, s.shape, 1) + (pair - mine) * tokens
+            s = jnp.where(token <= jnp.concatenate([idx_all] * repeats, axis=1), s, NEG_FILL)
+            m0[h], l0[h], acc0[h] = update(s, v_one, m0[h], l0[h], acc0[h])
+
+        @pl.when((z != 1) & (pair <= mine))
+        def _():
+            own(*operands())
 
         @pl.when(z == 1)
         def _():
-            for k in range(2):
-                s = scores(block, h, q_all[1 + k, h])
-                m1[k], l1[k], acc1[k] = update(block, h, s, m1[k], l1[k], acc1[k])
+            k, v_one = operands()
+            own(k, v_one)
+            for i in range(2):
+                s = dot(q_all[1 + i, h], k, 1, 1) * SCALE
+                m1[i], l1[i], acc1[i] = update(s, v_one, m1[i], l1[i], acc1[i])
 
     def source(j):
         below = j // columns
@@ -305,10 +310,9 @@
                     kv_copy(block, h, fw_send.at[j, h], sibling).wait_recv()
 
                 kv_copy(block, h, fw_send.at[j, h], sibling).start()
-                process(block, h)
                 twin = block + 1 - 2 * core
                 kv_copy(twin, h, fw_send.at[j, h], sibling).wait_recv()
-                process(twin, h)
+                process(block - core, h)
 
             return inner
 
@@ -318,7 +322,7 @@
         def _():
             for k in range(2):
                 po_src[k, h] = (acc1[k] / l1[k]).astype(jnp.bfloat16)
-                ps_src[k, h] = jnp.broadcast_to(m1[k] + jnp.log2(l1[k]), ps_src.shape[2:])
+                ps_src[k, h] = (m1[k] + jnp.log2(l1[k])).T[:8, :]
                 po_copy(k, h, me + (1 + k) * layer_size).start()
                 ps_copy(k, h, me + (1 + k) * layer_size).start()
 
@@ -326,10 +330,10 @@
 
     lax.fori_loop(0, kv_local, head_step, 0)
 
-    live_all = meta_ref[1:2, :] > 0
+    live_all = jnp.concatenate([wide_ref[1]] * HEADS_PER, axis=0) > 0
 
     def store(h, rows):
-        rows = jnp.where(live_all, rows, 0.0).T.astype(jnp.bfloat16)
+        rows = jnp.where(live_all, rows, 0.0).astype(jnp.bfloat16)
         for g in range(HEADS_PER):
             at = pl.multiple_of((h * HEADS_PER + g) * HEAD_DIM, HEAD_DIM)
             out_ref[:, pl.ds(at, HEAD_DIM)] = rows[g * slots : (g + 1) * slots, :]
@@ -343,7 +347,7 @@
         def _():
             po_copy(0, h, server).wait_recv()
             ps_copy(0, h, server).wait_recv()
-            stat = ps_dst[h, 0:1, :]
+            stat = jnp.concatenate([ps_dst[h]] * (HEAD_DIM // 8), axis=0).T
             top = jnp.maximum(m0[h], stat)
             own = jnp.exp2(m0[h] - top)
             far = jnp.exp2(stat - top)
@@ -412,7 +416,8 @@
     sine = jnp.sin(angles)
     cosine = jnp.concatenate([cosine, cosine], axis=1)
     sine = jnp.concatenate([-sine, sine], axis=1)
-    meta = jnp.stack([jnp.tile(indices, HEADS_PER), jnp.tile(live, HEADS_PER)])
+    meta = jnp.stack([indices, live])
+    wide = jnp.broadcast_to(meta[:, :, None], (2, slots, HEAD_DIM))
     rows = slots * HEADS_PER
     half = n // 2
     columns = n // LAYERS // 2
@@ -426,20 +431,20 @@
             jax.ShapeDtypeStruct(cached_values.shape, bf16),
             jax.ShapeDtypeStruct((1, slots), f32),
         ),
-        in_specs=[pl.BlockSpec(memory_space=pltpu.VMEM)] * 8,
+        in_specs=[pl.BlockSpec(memory_space=pltpu.VMEM)] * 9,
         out_specs=(pl.BlockSpec(memory_space=pltpu.VMEM),) * 4,
         scratch_shapes=[
             pltpu.VMEM((half, kv_local, 2, tokens, HEAD_DIM), bf16),
             pltpu.VMEM((3, kv_local, rows, HEAD_DIM), bf16),
-            pltpu.VMEM((kv_local, 1, rows), f32),
-            pltpu.VMEM((kv_local, 1, rows), f32),
-            pltpu.VMEM((kv_local, HEAD_DIM, rows), f32),
-            pltpu.VMEM((2, 1, rows), f32),
-            pltpu.VMEM((2, 1, rows), f32),
-            pltpu.VMEM((2, HEAD_DIM, rows), f32),
-            pltpu.VMEM((2, kv_local, HEAD_DIM, rows), bf16),
+            pltpu.VMEM((kv_local, rows, HEAD_DIM), f32),
+            pltpu.VMEM((kv_local, rows, HEAD_DIM), f32),
+            pltpu.VMEM((kv_local, rows, HEAD_DIM), f32),
+            pltpu.VMEM((2, rows, HEAD_DIM), f32),
+            pltpu.VMEM((2, rows, HEAD_DIM), f32),
+            pltpu.VMEM((2, rows, HEAD_DIM), f32),
+            pltpu.VMEM((2, kv_local, rows, HEAD_DIM), bf16),
             pltpu.VMEM((2, kv_local, 8, rows), f32),
-            pltpu.VMEM((kv_local, HEAD_DIM, rows), bf16),
+            pltpu.VMEM((kv_local, rows, HEAD_DIM), bf16),
             pltpu.VMEM((kv_local, 8, rows), f32),
             pltpu.VMEM((n_head, 8, HEAD_DIM), f32),
             dma((half, kv_local)),
@@ -462,7 +467,7 @@
             bytes_accessed=8 * tokens * width,
             transcendentals=half * kv_local * tokens * rows,
         ),
-    )(queries, cached_keys, cached_values, fresh_keys, fresh_values, cosine, sine, meta)
+    )(queries, cached_keys, cached_values, fresh_keys, fresh_values, cosine, sine, meta, wide)
 
 
 def solution(mesh):

time: 80.3 us -> 81.6 us (1.016)
  the two profiles are of different devices: /device:TPU:29 before, /device:TPU:24 now
where the time goes in v2:
time: 81.6 us; the launch traced here: 81.3 us
  Pallas kernels  70.6 us (87%)
  local copies, waits for them, and re-layouts  8.31 us (10%)
  between operations  1.36 us (2%)
  other arithmetic  0.96 us (1%)
    pallas_call x1, Pallas kernels, shards(): pl.pallas_call(functools.partial(kernel, n, n_head), out_shape=(jax.Shape...  70.6 us
    unnamed x18, local copies, waits for them, and re-layouts  7.66 us

profile of v2, /device:TPU:24, one launch (start us, length us, event | category | flops | bytes accessed | tf_op | source)
XLA Modules:
  0.0 81.3 jit_solution(8610829658574320797)
XLA Ops:
  1.3 0.0 copy-start.6
  1.3 0.6 copy-done.6
  1.9 0.6 dynamic_slice.4
  2.5 0.0 copy-start.5
  2.5 0.7 copy-done.5
  3.2 0.6 add_convert_fusion
  3.9 0.1 broadcast_in_dim.2.wide_ref
  3.9 0.2 fusion
  4.1 0.0 copy-start.3
  4.1 0.0 copy-start.4
  4.2 0.1 pad_maximum_fusion
  4.3 0.7 copy-done.3
  4.9 0.0 copy-done.4
  5.0 0.0 copy-start
  5.0 1.0 %copy-done = bf16[48,4096]{1,0:T(8,128)(2,1)S(1)} copy-done((bf16[48,4096]{1,0:T(8,128)(2,1)S(1)}, bf16[48,4096]{1,0:T(8,128)(2,1)}, u32[]{:S(2)}) %copy-start) | copy-done | bytes 393240
  6.0 0.0 copy-start.1
  6.0 1.0 %copy-done.1 = bf16[320,512]{1,0:T(8,128)(2,1)S(1)} copy-done((bf16[320,512]{1,0:T(8,128)(2,1)S(1)}, bf16[320,512]{1,0:T(8,128)(2,1)}, u32[]{:S(2)}) %copy-start.1) | copy-done | bytes 327704
  6.9 0.0 copy-start.2
  6.9 1.0 %copy-done.2 = bf16[320,512]{1,0:T(8,128)(2,1)S(1)} copy-done((bf16[320,512]{1,0:T(8,128)(2,1)S(1)}, bf16[320,512]{1,0:T(8,128)(2,1)}, u32[]{:S(2)}) %copy-start.2) | copy-done | bytes 327704
  7.9 70.6 %shard_map.111 = (bf16[48,4096]{1,0:T(8,128)(2,1)S(1)}, bf16[320,512]{1,0:T(8,128)(2,1)S(1)}, bf16[320,512]{1,0:T(8,128)(2,1)S(1)}, f32[1,48]{1,0:T(1,128)S(1)}) custom-call(bf16[48,4096]{1,0:T(8,128)(2,1)S(1)} %copy-done, bf16[320,512]{1,0:T(8,128)(2,1)S(1)} %copy-done.1, bf16[320,512]{1,0:T(8,128)(2,1)S(1)} %copy-done.2, bf16[48,512]{1,0:T(8,128)(2,1)S(1)} %copy-done.3, ...), custom_call_target="tpu_custom_call" | custom-call | flops 2013265920 | bytes 1310720 | tf_op jit(solution)/shard_map/pallas_call | solution.py:426
  78.6 0.7 copy.17
  79.3 0.7 copy.18
  80.0 0.7 copy.19
  80.8 0.5 copy.20
  (3 shorter events, 0.0 us)
Async XLA Ops:
  1.3 0.7 copy-start.6
  2.5 0.7 copy-start.5
  4.1 0.8 copy-start.3
  4.1 0.8 %copy-start.4 = (bf16[48,512]{1,0:T(8,128)(2,1)S(1)}, bf16[48,512]{1,0:T(8,128)(2,1)}, u32[]{:S(2)}) copy-start(bf16[48,512]{1,0:T(8,128)(2,1)} %fv_ref.1) | copy-start | bytes 147460
  5.0 1.0 %copy-start = (bf16[48,4096]{1,0:T(8,128)(2,1)S(1)}, bf16[48,4096]{1,0:T(8,128)(2,1)}, u32[]{:S(2)}) copy-start(bf16[48,4096]{1,0:T(8,128)(2,1)} %q_ref.1) | copy-start | bytes 1179652
  6.0 1.0 %copy-start.1 = (bf16[320,512]{1,0:T(8,128)(2,1)S(1)}, bf16[320,512]{1,0:T(8,128)(2,1)}, u32[]{:S(2)}) copy-start(bf16[320,512]{1,0:T(8,128)(2,1)} %ck_ref.1) | copy-start | bytes 983044
  6.9 1.0 %copy-start.2 = (bf16[320,512]{1,0:T(8,128)(2,1)S(1)}, bf16[320,512]{1,0:T(8,128)(2,1)}, u32[]{:S(2)}) copy-start(bf16[320,512]{1,0:T(8,128)(2,1)} %cv_ref.1) | copy-start | bytes 983044

commit v3 on v2

--- a/solution.py
+++ b/solution.py
@@ -135,6 +135,44 @@
     def _():
         greet(server)
 
+    def copy(src, dst, send, recv, target):
+        return pltpu.make_async_remote_copy(
+            src_ref=src,
+            dst_ref=dst,
+            send_sem=send,
+            recv_sem=recv,
+            device_id={"ctx": target},
+            device_id_type=MESH,
+        )
+
+    def kv_copy(block, h, send, target):
+        return copy(kv_buf.at[block, h], kv_buf.at[block, h], send, kv_recv.at[block, h], target)
+
+    def q_copy(h):
+        which = jnp.where(z >= 2, z - 1, 1)
+        return copy(
+            q_all.at[0, h], q_all.at[which, h], q_send.at[h], q_recv.at[which - 1, h], server
+        )
+
+    def po_copy(k, h, target):
+        return copy(po_src.at[k, h], po_dst.at[h], po_send.at[k, h], po_recv.at[h], target)
+
+    def ps_copy(k, h, target):
+        return copy(ps_src.at[k, h], ps_dst.at[h], ps_send.at[k, h], ps_recv.at[h], target)
+
+    def each_send(h, act):
+        for k in range(columns):
+            @pl.when(odd == 0)
+            def _():
+                act(kv_copy(mine, h, kv_send.at[columns + k, h],
+                            other_start + lax.rem(y + k, columns) * 2 + core))
+        for k in range(1, columns):
+            there = lax.rem(y + k, columns)
+
+            @pl.when((odd == 1) | (there > y))
+            def _():
+                act(kv_copy(mine, h, kv_send.at[k, h], layer_start + there * 2 + core))
+
     idx_row = meta_ref[0:1, :slots]
     live_row = meta_ref[1:2, :slots]
     base_cos = cos_ref[slots : slots + 1, :]
@@ -148,6 +186,7 @@
     hit_live = hit_live.astype(jnp.bfloat16)
     ones = jnp.ones((8, HEAD_DIM), jnp.float32)
     drift = jnp.zeros((8, slots), jnp.float32)
+    turned_rows, fresh_rows = [], []
     for h in range(kv_local):
         cols = slice(h * HEAD_DIM, (h + 1) * HEAD_DIM)
         turned = turn(ck_ref[:, cols], base_cos, base_sin)
@@ -164,6 +203,16 @@
         jv_ref[:, cols] = vals
         kv_buf[mine, h, 0] = keys
         kv_buf[mine, h, 1] = vals
+        if h == 0:
+            extra = jnp.where(z == 0, 0, jnp.where(z == 1, 2, 1))
+            pl.semaphore_wait(barrier, 2 * columns + n_head - 1 + extra)
+        each_send(h, lambda c: c.start())
+        turned_rows.append(turned)
+        fresh_rows.append(fresh)
+    for h in range(kv_local):
+        cols = slice(h * HEAD_DIM, (h + 1) * HEAD_DIM)
+        turned, fresh = turned_rows[h], fresh_rows[h]
+        cached_v, fresh_v = cv_ref[:, cols], fv_ref[:, cols]
         key_gap = fresh.astype(jnp.float32) - dot(hit, turned, 0, 0)
         val_gap = fresh_v.astype(jnp.float32) - dot(hit, cached_v, 0, 0)
         drift += dot(
@@ -174,59 +223,13 @@
             q_all[0, h, g * slots : (g + 1) * slots, :] = turn(
                 q_ref[:, at : at + HEAD_DIM], slot_cos, slot_sin
             )
+
+        @pl.when(z >= 2)
+        def _():
+            q_copy(h).start()
+
     d_buf[my_head] = jnp.zeros(d_buf.shape[1:], jnp.float32)
     d_buf[my_head, :, :slots] = drift
-
-    extra = jnp.where(z == 0, 0, jnp.where(z == 1, 2, 1))
-    pl.semaphore_wait(barrier, 2 * columns + n_head - 1 + extra)
-
-    def copy(src, dst, send, recv, target):
-        return pltpu.make_async_remote_copy(
-            src_ref=src,
-            dst_ref=dst,
-            send_sem=send,
-            recv_sem=recv,
-            device_id={"ctx": target},
-            device_id_type=MESH,
-        )
-
-    def kv_copy(block, h, send, target):
-        return copy(kv_buf.at[block, h], kv_buf.at[block, h], send, kv_recv.at[block, h], target)
-
-    def q_copy(h):
-        which = jnp.where(z >= 2, z - 1, 1)
-        return copy(
-            q_all.at[0, h], q_all.at[which, h], q_send.at[h], q_recv.at[which - 1, h], server
-        )
-
-    def po_copy(k, h, target):
-        return copy(po_src.at[k, h], po_dst.at[h], po_send.at[k, h], po_recv.at[h], target)
-
-    def ps_copy(k, h, target):
-        return copy(ps_src.at[k, h], ps_dst.at[h], ps_send.at[k, h], ps_recv.at[h], target)
-
-    def each_send(h, act):
-        for k in range(columns):
-            @pl.when(odd == 0)
-            def _():
-                act(kv_copy(mine, h, kv_send.at[columns + k, h],
-                            other_start + lax.rem(y + k, columns) * 2 + core))
-        for k in range(1, columns):
-            there = lax.rem(y + k, columns)
-
-            @pl.when((odd == 1) | (there > y))
-            def _():
-                act(kv_copy(mine, h, kv_send.at[k, h], layer_start + there * 2 + core))
-
-        @pl.when(z >= 2)
-        def _():
-            act(q_copy(h))
-
-    def start_sends(h, carry):
-        each_send(h, lambda c: c.start())
-        return carry
-
-    lax.fori_loop(0, kv_local, start_sends, 0)
 
     def drift_copy(k):
         target = lax.rem(my_head + k, n_head)
@@ -285,40 +288,52 @@
         need = ((odd == 1) | (below == 0)) & ((odd == 1) | (there <= y))
         return block, need
 
-    def head_step(h, carry):
-        m0[h] = jnp.full(m0.shape[1:], NEG_FILL, jnp.float32)
-        l0[h] = jnp.zeros(l0.shape[1:], jnp.float32)
-        acc0[h] = jnp.zeros(acc0.shape[1:], jnp.float32)
-
-        @pl.when(z == 1)
-        def _():
-            m1[...] = jnp.full(m1.shape, NEG_FILL, jnp.float32)
-            l1[...] = jnp.zeros(l1.shape, jnp.float32)
-            acc1[...] = jnp.zeros(acc1.shape, jnp.float32)
-            for k in range(2):
-                copy(
-                    q_all.at[0, h], q_all.at[1 + k, h], q_send.at[h], q_recv.at[k, h], server
-                ).wait_recv()
-
-        def block_step(j, inner):
-            block, need = source(j)
-
-            @pl.when(need)
+    steps = 2 * columns
+
+    def advance(t):
+        h, j = t // steps, t % steps
+        block, need = source(j)
+
+        @pl.when(need)
+        def _():
+            @pl.when(block != mine)
             def _():
-                @pl.when(block != mine)
-                def _():
-                    kv_copy(block, h, fw_send.at[j, h], sibling).wait_recv()
-
-                kv_copy(block, h, fw_send.at[j, h], sibling).start()
-                twin = block + 1 - 2 * core
-                kv_copy(twin, h, fw_send.at[j, h], sibling).wait_recv()
-                process(block - core, h)
-
-            return inner
-
-        lax.fori_loop(0, 2 * columns, block_step, 0)
-
-        @pl.when(z == 1)
+                kv_copy(block, h, fw_send.at[j, h], sibling).wait_recv()
+
+            kv_copy(block, h, fw_send.at[j, h], sibling).start()
+
+    def attend_step(t, carry):
+        h, j = t // steps, t % steps
+
+        @pl.when(t + 1 < kv_local * steps)
+        def _():
+            advance(t + 1)
+
+        @pl.when(j == 0)
+        def _():
+            m0[h] = jnp.full(m0.shape[1:], NEG_FILL, jnp.float32)
+            l0[h] = jnp.zeros(l0.shape[1:], jnp.float32)
+            acc0[h] = jnp.zeros(acc0.shape[1:], jnp.float32)
+
+            @pl.when(z == 1)
+            def _():
+                m1[...] = jnp.full(m1.shape, NEG_FILL, jnp.float32)
+                l1[...] = jnp.zeros(l1.shape, jnp.float32)
+                acc1[...] = jnp.zeros(acc1.shape, jnp.float32)
+                for k in range(2):
+                    copy(
+                        q_all.at[0, h], q_all.at[1 + k, h], q_send.at[h], q_recv.at[k, h], server
+                    ).wait_recv()
+
+        block, need = source(j)
+
+        @pl.when(need)
+        def _():
+            twin = block + 1 - 2 * core
+            kv_copy(twin, h, fw_send.at[j, h], sibling).wait_recv()
+            process(block - core, h)
+
+        @pl.when((z == 1) & (j == steps - 1))
         def _():
             for k in range(2):
                 po_src[k, h] = (acc1[k] / l1[k]).astype(jnp.bfloat16)
@@ -328,7 +343,8 @@
 
         return carry
 
-    lax.fori_loop(0, kv_local, head_step, 0)
+    advance(jnp.int32(0))
+    lax.fori_loop(0, kv_local * steps, attend_step, 0)
 
     live_all = jnp.concatenate([wide_ref[1]] * HEADS_PER, axis=0) > 0
 
@@ -369,6 +385,10 @@
 
     def drain(h, carry):
         each_send(h, lambda c: c.wait_send())
+
+        @pl.when(z >= 2)
+        def _():
+            q_copy(h).wait_send()
 
         def drain_block(j, inner):
             block, need = source(j)

time: 81.6 us -> 64.9 us (0.80)
  Pallas kernels: 70.6 us -> 54 us
    pallas_call x1, Pallas kernels: 70.6 us -> 54 us  [shards(): pl.pallas_call(functools.partial(kernel, n, n_head), out_shape=(jax.Shape...]
where the time goes in v3:
time: 64.9 us; the launch traced here: 64.6 us
  Pallas kernels  54 us (83%)
  local copies, waits for them, and re-layouts  8.31 us (13%)
  between operations  1.36 us (2%)
  other arithmetic  0.96 us (1%)
    pallas_call x1, Pallas kernels, shards(): pl.pallas_call(functools.partial(kernel, n, n_head), out_shape=(jax.Shape...  54 us
    unnamed x18, local copies, waits for them, and re-layouts  7.66 us

profile of v3, /device:TPU:24, one launch (start us, length us, event | category | flops | bytes accessed | tf_op | source)
XLA Modules:
  0.0 64.6 jit_solution(18445192693861625213)
XLA Ops:
  1.3 0.0 copy-start.6
  1.3 0.6 copy-done.6
  1.9 0.6 dynamic_slice.4
  2.5 0.0 copy-start.5
  2.5 0.7 %copy-done.5 = s32[1,48]{1,0:T(1,128)S(1)} copy-done((s32[1,48]{1,0:T(1,128)S(1)}, s32[1,48]{1,0:T(1,128)}, u32[]{:S(2)}) %copy-start.5) | copy-done | bytes 216
  3.2 0.6 %add_convert_fusion = f32[56]{0:T(128)S(1)} fusion(s32[48]{0:T(128)S(1)} %bitcast.4, s32[]{:T(128)} %bitcast), kind=kLoop, calls=%fused_computation.9 | loop fusion | flops 112 | bytes 420 | tf_op jit(solution)/shard_map/convert_element_type | solution.py:434
  3.9 0.1 broadcast_in_dim.2.wide_ref
  3.9 0.2 fusion
  4.1 0.0 copy-start.3
  4.1 0.0 copy-start.4
  4.2 0.1 pad_maximum_fusion
  4.3 0.7 %copy-done.3 = bf16[48,512]{1,0:T(8,128)(2,1)S(1)} copy-done((bf16[48,512]{1,0:T(8,128)(2,1)S(1)}, bf16[48,512]{1,0:T(8,128)(2,1)}, u32[]{:S(2)}) %copy-start.3) | copy-done | bytes 49176
  4.9 0.0 copy-done.4
  5.0 0.0 copy-start
  5.0 1.0 %copy-done = bf16[48,4096]{1,0:T(8,128)(2,1)S(1)} copy-done((bf16[48,4096]{1,0:T(8,128)(2,1)S(1)}, bf16[48,4096]{1,0:T(8,128)(2,1)}, u32[]{:S(2)}) %copy-start) | copy-done | bytes 393240
  6.0 0.0 copy-start.1
  6.0 1.0 %copy-done.1 = bf16[320,512]{1,0:T(8,128)(2,1)S(1)} copy-done((bf16[320,512]{1,0:T(8,128)(2,1)S(1)}, bf16[320,512]{1,0:T(8,128)(2,1)}, u32[]{:S(2)}) %copy-start.1) | copy-done | bytes 327704
  6.9 0.0 copy-start.2
  6.9 1.0 %copy-done.2 = bf16[320,512]{1,0:T(8,128)(2,1)S(1)} copy-done((bf16[320,512]{1,0:T(8,128)(2,1)S(1)}, bf16[320,512]{1,0:T(8,128)(2,1)}, u32[]{:S(2)}) %copy-start.2) | copy-done | bytes 327704
  7.9 54.0 %shard_map.111 = (bf16[48,4096]{1,0:T(8,128)(2,1)S(1)}, bf16[320,512]{1,0:T(8,128)(2,1)S(1)}, bf16[320,512]{1,0:T(8,128)(2,1)S(1)}, f32[1,48]{1,0:T(1,128)S(1)}) custom-call(bf16[48,4096]{1,0:T(8,128)(2,1)S(1)} %copy-done, bf16[320,512]{1,0:T(8,128)(2,1)S(1)} %copy-done.1, bf16[320,512]{1,0:T(8,128)(2,1)S(1)} %copy-done.2, bf16[48,512]{1,0:T(8,128)(2,1)S(1)} %copy-done.3, ...), custom_call_target="tpu_custom_call" | custom-call | flops 2013265920 | bytes 1310720 | tf_op jit(solution)/shard_map/pallas_call | solution.py:446
  61.9 0.7 %copy.17 = bf16[48,4096]{1,0:T(8,128)(2,1)} copy(bf16[48,4096]{1,0:T(8,128)(2,1)S(1)} %get-tuple-element.13) | data formatting | bytes 786432
  62.6 0.7 %copy.18 = bf16[320,512]{1,0:T(8,128)(2,1)} copy(bf16[320,512]{1,0:T(8,128)(2,1)S(1)} %get-tuple-element.14) | data formatting | bytes 655360
  63.4 0.7 %copy.19 = bf16[320,512]{1,0:T(8,128)(2,1)} copy(bf16[320,512]{1,0:T(8,128)(2,1)S(1)} %get-tuple-element.15) | data formatting | bytes 655360
  64.1 0.5 copy.20
  (3 shorter events, 0.0 us)
Async XLA Ops:
  1.3 0.7 %copy-start.6 = (s32[16]{0:T(128)S(1)}, s32[16]{0:T(128)}, u32[]{:S(2)}) copy-start(s32[16]{0:T(128)} %param.15) | copy-start | bytes 196
  2.5 0.7 %copy-start.5 = (s32[1,48]{1,0:T(1,128)S(1)}, s32[1,48]{1,0:T(1,128)}, u32[]{:S(2)}) copy-start(s32[1,48]{1,0:T(1,128)} %param.13) | copy-start | bytes 580
  4.1 0.8 %copy-start.3 = (bf16[48,512]{1,0:T(8,128)(2,1)S(1)}, bf16[48,512]{1,0:T(8,128)(2,1)}, u32[]{:S(2)}) copy-start(bf16[48,512]{1,0:T(8,128)(2,1)} %fk_ref.1) | copy-start | bytes 147460
  4.1 0.8 %copy-start.4 = (bf16[48,512]{1,0:T(8,128)(2,1)S(1)}, bf16[48,512]{1,0:T(8,128)(2,1)}, u32[]{:S(2)}) copy-start(bf16[48,512]{1,0:T(8,128)(2,1)} %fv_ref.1) | copy-start | bytes 147460
  5.0 1.0 %copy-start = (bf16[48,4096]{1,0:T(8,128)(2,1)S(1)}, bf16[48,4096]{1,0:T(8,128)(2,1)}, u32[]{:S(2)}) copy-start(bf16[48,4096]{1,0:T(8,128)(2,1)} %q_ref.1) | copy-start | bytes 1179652
  6.0 1.0 %copy-start.1 = (bf16[320,512]{1,0:T(8,128)(2,1)S(1)}, bf16[320,512]{1,0:T(8,128)(2,1)}, u32[]{:S(2)}) copy-start(bf16[320,512]{1,0:T(8,128)(2,1)} %ck_ref.1) | copy-start | bytes 983044
  6.9 1.0 %copy-start.2 = (bf16[320,512]{1,0:T(8,128)(2,1)S(1)}, bf16[320,512]{1,0:T(8,128)(2,1)}, u32[]{:S(2)}) copy-start(bf16[320,512]{1,0:T(8,128)(2,1)} %cv_ref.1) | copy-start | bytes 983044

commit v4 on v3

--- a/solution.py
+++ b/solution.py
@@ -105,7 +105,9 @@
     below_start = layer_start - layer_size
     half_start = me - mine
     sibling = half_start + mine + 1 - 2 * core
-    server = layer_size + me % layer_size
+    partner = lax.rem(me + half, n)
+    serves = z < 2
+    full = z != 2
 
     barrier = pltpu.get_barrier_semaphore()
 
@@ -126,14 +128,7 @@
             device_id_type=MESH,
         )
 
-    @pl.when(z == 1)
-    def _():
-        greet(me + layer_size)
-        greet(me + 2 * layer_size)
-
-    @pl.when(z >= 2)
-    def _():
-        greet(server)
+    greet(partner)
 
     def copy(src, dst, send, recv, target):
         return pltpu.make_async_remote_copy(
@@ -149,27 +144,24 @@
         return copy(kv_buf.at[block, h], kv_buf.at[block, h], send, kv_recv.at[block, h], target)
 
     def q_copy(h):
-        which = jnp.where(z >= 2, z - 1, 1)
-        return copy(
-            q_all.at[0, h], q_all.at[which, h], q_send.at[h], q_recv.at[which - 1, h], server
-        )
-
-    def po_copy(k, h, target):
-        return copy(po_src.at[k, h], po_dst.at[h], po_send.at[k, h], po_recv.at[h], target)
-
-    def ps_copy(k, h, target):
-        return copy(ps_src.at[k, h], ps_dst.at[h], ps_send.at[k, h], ps_recv.at[h], target)
+        return copy(q_all.at[0, h], q_all.at[1, h], q_send.at[h], q_recv.at[h], partner)
+
+    def po_copy(h):
+        return copy(po_src.at[h], po_dst.at[h], po_send.at[h], po_recv.at[h], partner)
+
+    def ps_copy(h):
+        return copy(ps_src.at[h], ps_dst.at[h], ps_send.at[h], ps_recv.at[h], partner)
 
     def each_send(h, act):
         for k in range(columns):
-            @pl.when(odd == 0)
+            @pl.when(z != 3)
             def _():
                 act(kv_copy(mine, h, kv_send.at[columns + k, h],
                             other_start + lax.rem(y + k, columns) * 2 + core))
         for k in range(1, columns):
             there = lax.rem(y + k, columns)
 
-            @pl.when((odd == 1) | (there > y))
+            @pl.when(full | (there > y))
             def _():
                 act(kv_copy(mine, h, kv_send.at[k, h], layer_start + there * 2 + core))
 
@@ -204,8 +196,7 @@
         kv_buf[mine, h, 0] = keys
         kv_buf[mine, h, 1] = vals
         if h == 0:
-            extra = jnp.where(z == 0, 0, jnp.where(z == 1, 2, 1))
-            pl.semaphore_wait(barrier, 2 * columns + n_head - 1 + extra)
+            pl.semaphore_wait(barrier, 2 * columns + n_head)
         each_send(h, lambda c: c.start())
         turned_rows.append(turned)
         fresh_rows.append(fresh)
@@ -269,23 +260,29 @@
             s = jnp.where(token <= jnp.concatenate([idx_all] * repeats, axis=1), s, NEG_FILL)
             m0[h], l0[h], acc0[h] = update(s, v_one, m0[h], l0[h], acc0[h])
 
-        @pl.when((z != 1) & (pair <= mine))
+        def served(k, v_one):
+            s = dot(q_all[1, h], k, 1, 1) * SCALE
+            m1[...], l1[...], acc1[...] = update(s, v_one, m1[...], l1[...], acc1[...])
+
+        @pl.when((z >= 2) & (pair <= mine))
         def _():
             own(*operands())
 
-        @pl.when(z == 1)
+        @pl.when(serves & (pair <= mine))
         def _():
             k, v_one = operands()
             own(k, v_one)
-            for i in range(2):
-                s = dot(q_all[1 + i, h], k, 1, 1) * SCALE
-                m1[i], l1[i], acc1[i] = update(s, v_one, m1[i], l1[i], acc1[i])
+            served(k, v_one)
+
+        @pl.when(serves & (pair > mine))
+        def _():
+            served(*operands())
 
     def source(j):
         below = j // columns
         there = lax.rem(y + j % columns, columns)
-        block = (odd - below) * layer_size + there * 2 + core
-        need = ((odd == 1) | (below == 0)) & ((odd == 1) | (there <= y))
+        block = jnp.where(below == 0, odd, 1 - odd) * layer_size + there * 2 + core
+        need = full | ((below == 0) & (there <= y))
         return block, need
 
     steps = 2 * columns
@@ -315,15 +312,12 @@
             l0[h] = jnp.zeros(l0.shape[1:], jnp.float32)
             acc0[h] = jnp.zeros(acc0.shape[1:], jnp.float32)
 
-            @pl.when(z == 1)
+            @pl.when(serves)
             def _():
                 m1[...] = jnp.full(m1.shape, NEG_FILL, jnp.float32)
                 l1[...] = jnp.zeros(l1.shape, jnp.float32)
                 acc1[...] = jnp.zeros(acc1.shape, jnp.float32)
-                for k in range(2):
-                    copy(
-                        q_all.at[0, h], q_all.at[1 + k, h], q_send.at[h], q_recv.at[k, h], server
-                    ).wait_recv()
+                q_copy(h).wait_recv()
 
         block, need = source(j)
 
@@ -333,13 +327,12 @@
             kv_copy(twin, h, fw_send.at[j, h], sibling).wait_recv()
             process(block - core, h)
 
-        @pl.when((z == 1) & (j == steps - 1))
-        def _():
-            for k in range(2):
-                po_src[k, h] = (acc1[k] / l1[k]).astype(jnp.bfloat16)
-                ps_src[k, h] = (m1[k] + jnp.log2(l1[k])).T[:8, :]
-                po_copy(k, h, me + (1 + k) * layer_size).start()
-                ps_copy(k, h, me + (1 + k) * layer_size).start()
+        @pl.when(serves & (j == steps - 1))
+        def _():
+            po_src[h] = (acc1[...] / l1[...]).astype(jnp.bfloat16)
+            ps_src[h] = (m1[...] + jnp.log2(l1[...])).T[:8, :]
+            po_copy(h).start()
+            ps_copy(h).start()
 
         return carry
 
@@ -361,8 +354,8 @@
 
         @pl.when(z >= 2)
         def _():
-            po_copy(0, h, server).wait_recv()
-            ps_copy(0, h, server).wait_recv()
+            po_copy(h).wait_recv()
+            ps_copy(h).wait_recv()
             stat = jnp.concatenate([ps_dst[h]] * (HEAD_DIM // 8), axis=0).T
             top = jnp.maximum(m0[h], stat)
             own = jnp.exp2(m0[h] - top)
@@ -401,11 +394,10 @@
 
         lax.fori_loop(0, 2 * columns, drain_block, 0)
 
-        @pl.when(z == 1)
-        def _():
-            for k in range(2):
-                po_copy(k, h, me + (1 + k) * layer_size).wait_send()
-                ps_copy(k, h, me + (1 + k) * layer_size).wait_send()
+        @pl.when(serves)
+        def _():
+            po_copy(h).wait_send()
+            ps_copy(h).wait_send()
 
         return carry
 
@@ -455,15 +447,15 @@
         out_specs=(pl.BlockSpec(memory_space=pltpu.VMEM),) * 4,
         scratch_shapes=[
             pltpu.VMEM((half, kv_local, 2, tokens, HEAD_DIM), bf16),
-            pltpu.VMEM((3, kv_local, rows, HEAD_DIM), bf16),
+            pltpu.VMEM((2, kv_local, rows, HEAD_DIM), bf16),
             pltpu.VMEM((kv_local, rows, HEAD_DIM), f32),
             pltpu.VMEM((kv_local, rows, HEAD_DIM), f32),
             pltpu.VMEM((kv_local, rows, HEAD_DIM), f32),
-            pltpu.VMEM((2, rows, HEAD_DIM), f32),
-            pltpu.VMEM((2, rows, HEAD_DIM), f32),
-            pltpu.VMEM((2, rows, HEAD_DIM), f32),
-            pltpu.VMEM((2, kv_local, rows, HEAD_DIM), bf16),
-            pltpu.VMEM((2, kv_local, 8, rows), f32),
+            pltpu.VMEM((rows, HEAD_DIM), f32),
+            pltpu.VMEM((rows, HEAD_DIM), f32),
+            pltpu.VMEM((rows, HEAD_DIM), f32),
+            pltpu.VMEM((kv_local, rows, HEAD_DIM), bf16),
+            pltpu.VMEM((kv_local, 8, rows), f32),
             pltpu.VMEM((kv_local, rows, HEAD_DIM), bf16),
             pltpu.VMEM((kv_local, 8, rows), f32),
             pltpu.VMEM((n_head, 8, HEAD_DIM), f32),
@@ -471,10 +463,10 @@
             dma((2 * columns, kv_local)),
             dma((2 * columns, kv_local)),
             dma((kv_local,)),
-            dma((2, kv_local)),
-            dma((2, kv_local)),
             dma((kv_local,)),
-            dma((2, kv_local)),
+            dma((kv_local,)),
+            dma((kv_local,)),
+            dma((kv_local,)),
             dma((kv_local,)),
             dma((n_head,)),
             dma((n_head,)),

time: 64.9 us -> 60.5 us (0.932)
  the two profiles are of different devices: /device:TPU:24 before, /device:TPU:0 now
where the time goes in v4:
time: 60.5 us; the launch traced here: 60.1 us
  Pallas kernels  49.5 us (82%)
  local copies, waits for them, and re-layouts  8.31 us (14%)
  between operations  1.36 us (2%)
  other arithmetic  0.96 us (2%)
    pallas_call x1, Pallas kernels, shards(): pl.pallas_call(functools.partial(kernel, n, n_head), out_shape=(jax.Shape...  49.5 us
    unnamed x18, local copies, waits for them, and re-layouts  7.66 us

profile of v4, /device:TPU:0, one launch (start us, length us, event | category | flops | bytes accessed | tf_op | source)
XLA Modules:
  0.0 60.1 jit_solution(3659166885050364793)
XLA Ops:
  1.3 0.0 copy-start.6
  1.3 0.6 %copy-done.6 = s32[16]{0:T(128)S(1)} copy-done((s32[16]{0:T(128)S(1)}, s32[16]{0:T(128)}, u32[]{:S(2)}) %copy-start.6) | copy-done | bytes 88
  1.9 0.6 dynamic_slice.4
  2.5 0.0 copy-start.5
  2.5 0.7 %copy-done.5 = s32[1,48]{1,0:T(1,128)S(1)} copy-done((s32[1,48]{1,0:T(1,128)S(1)}, s32[1,48]{1,0:T(1,128)}, u32[]{:S(2)}) %copy-start.5) | copy-done | bytes 216
  3.2 0.6 %add_convert_fusion = f32[56]{0:T(128)S(1)} fusion(s32[48]{0:T(128)S(1)} %bitcast.4, s32[]{:T(128)} %bitcast), kind=kLoop, calls=%fused_computation.9 | loop fusion | flops 112 | bytes 420 | tf_op jit(solution)/shard_map/convert_element_type | solution.py:426
  3.9 0.1 broadcast_in_dim.2.wide_ref
  3.9 0.2 fusion
  4.1 0.0 copy-start.3
  4.1 0.0 copy-start.4
  4.2 0.1 pad_maximum_fusion
  4.3 0.7 %copy-done.3 = bf16[48,512]{1,0:T(8,128)(2,1)S(1)} copy-done((bf16[48,512]{1,0:T(8,128)(2,1)S(1)}, bf16[48,512]{1,0:T(8,128)(2,1)}, u32[]{:S(2)}) %copy-start.3) | copy-done | bytes 49176
  4.9 0.0 copy-done.4
  5.0 0.0 copy-start
  5.0 1.0 %copy-done = bf16[48,4096]{1,0:T(8,128)(2,1)S(1)} copy-done((bf16[48,4096]{1,0:T(8,128)(2,1)S(1)}, bf16[48,4096]{1,0:T(8,128)(2,1)}, u32[]{:S(2)}) %copy-start) | copy-done | bytes 393240
  6.0 0.0 copy-start.1
  6.0 1.0 %copy-done.1 = bf16[320,512]{1,0:T(8,128)(2,1)S(1)} copy-done((bf16[320,512]{1,0:T(8,128)(2,1)S(1)}, bf16[320,512]{1,0:T(8,128)(2,1)}, u32[]{:S(2)}) %copy-start.1) | copy-done | bytes 327704
  6.9 0.0 copy-start.2
  6.9 1.0 %copy-done.2 = bf16[320,512]{1,0:T(8,128)(2,1)S(1)} copy-done((bf16[320,512]{1,0:T(8,128)(2,1)S(1)}, bf16[320,512]{1,0:T(8,128)(2,1)}, u32[]{:S(2)}) %copy-start.2) | copy-done | bytes 327704
  7.9 49.5 %shard_map.111 = (bf16[48,4096]{1,0:T(8,128)(2,1)S(1)}, bf16[320,512]{1,0:T(8,128)(2,1)S(1)}, bf16[320,512]{1,0:T(8,128)(2,1)S(1)}, f32[1,48]{1,0:T(1,128)S(1)}) custom-call(bf16[48,4096]{1,0:T(8,128)(2,1)S(1)} %copy-done, bf16[320,512]{1,0:T(8,128)(2,1)S(1)} %copy-done.1, bf16[320,512]{1,0:T(8,128)(2,1)S(1)} %copy-done.2, bf16[48,512]{1,0:T(8,128)(2,1)S(1)} %copy-done.3, ...), custom_call_target="tpu_custom_call" | custom-call | flops 2013265920 | bytes 1310720 | tf_op jit(solution)/shard_map/pallas_call | solution.py:438
  57.4 0.7 %copy.17 = bf16[48,4096]{1,0:T(8,128)(2,1)} copy(bf16[48,4096]{1,0:T(8,128)(2,1)S(1)} %get-tuple-element.13) | data formatting | bytes 786432
  58.2 0.7 %copy.18 = bf16[320,512]{1,0:T(8,128)(2,1)} copy(bf16[320,512]{1,0:T(8,128)(2,1)S(1)} %get-tuple-element.14) | data formatting | bytes 655360
  58.9 0.7 %copy.19 = bf16[320,512]{1,0:T(8,128)(2,1)} copy(bf16[320,512]{1,0:T(8,128)(2,1)S(1)} %get-tuple-element.15) | data formatting | bytes 655360
  59.6 0.5 copy.20
  (3 shorter events, 0.0 us)
Async XLA Ops:
  1.3 0.7 %copy-start.6 = (s32[16]{0:T(128)S(1)}, s32[16]{0:T(128)}, u32[]{:S(2)}) copy-start(s32[16]{0:T(128)} %param.15) | copy-start | bytes 196
  2.5 0.7 %copy-start.5 = (s32[1,48]{1,0:T(1,128)S(1)}, s32[1,48]{1,0:T(1,128)}, u32[]{:S(2)}) copy-start(s32[1,48]{1,0:T(1,128)} %param.13) | copy-start | bytes 580
  4.1 0.8 %copy-start.3 = (bf16[48,512]{1,0:T(8,128)(2,1)S(1)}, bf16[48,512]{1,0:T(8,128)(2,1)}, u32[]{:S(2)}) copy-start(bf16[48,512]{1,0:T(8,128)(2,1)} %fk_ref.1) | copy-start | bytes 147460
  4.1 0.8 %copy-start.4 = (bf16[48,512]{1,0:T(8,128)(2,1)S(1)}, bf16[48,512]{1,0:T(8,128)(2,1)}, u32[]{:S(2)}) copy-start(bf16[48,512]{1,0:T(8,128)(2,1)} %fv_ref.1) | copy-start | bytes 147460
  5.0 1.0 %copy-start = (bf16[48,4096]{1,0:T(8,128)(2,1)S(1)}, bf16[48,4096]{1,0:T(8,128)(2,1)}, u32[]{:S(2)}) copy-start(bf16[48,4096]{1,0:T(8,128)(2,1)} %q_ref.1) | copy-start | bytes 1179652
  6.0 1.0 %copy-start.1 = (bf16[320,512]{1,0:T(8,128)(2,1)S(1)}, bf16[320,512]{1,0:T(8,128)(2,1)}, u32[]{:S(2)}) copy-start(bf16[320,512]{1,0:T(8,128)(2,1)} %ck_ref.1) | copy-start | bytes 983044
  6.9 1.0 %copy-start.2 = (bf16[320,512]{1,0:T(8,128)(2,1)S(1)}, bf16[320,512]{1,0:T(8,128)(2,1)}, u32[]{:S(2)}) copy-start(bf16[320,512]{1,0:T(8,128)(2,1)} %cv_ref.1) | copy-start | bytes 983044
